TPU v7x, 256 devices: a whole 4x4x8 slice. The times are simulated.
256 devices in a mesh: col: 32 (over z, x_lo, core), lev: 8 (over y, x_hi).
Axes of the slice: x: 4 (x_hi: 2, x_lo: 2; x = x_hi * 2 + x_lo), y: 4, z: 8, core: 2. Of those that a mesh axis runs over, the one named last changes fastest.
Arguments:
- ensemble: float32 [80, 4, 16, 16384], P(None, None, 'lev', 'col'), may hold values from -60 to 60
- obs_weight: float32 [4, 4, 16, 1024], P(None, None, 'lev'), may hold values from -0.75 to 0.75
- obs_value: float32 [4, 1024], replicated, may hold values from -6 to 6
- obs_tile: int32 [4, 1024, 1], replicated, may hold values from 0 to 31; in each aligned block of 1024 rows (0 to 1023, 1024 to 2047, ..., all dimensions but the last counted through in order) at most 128 rows name the same one
- obs_offset: int32 [4, 1024], replicated, may hold values from 0 to 511
- obs_gain: bfloat16 [4, 1024, 1024], P(None, 'lev'), may hold values from -0.1 to 0.3
- localize: bfloat16 [4, 1024, 16384], P(None, None, 'col'), may hold values from 0.049804688 to 1
Outputs:
- analysis: float32 [80, 4, 16, 16384], P(None, None, 'lev', 'col')
Inputs may be any that keep to these rules, and one draw needn't show every extreme that they name: `obs_tile`: in each batch at most 128 observations lie in one column tile; in some batch some tile holds exactly 128.
All inputs are finite; a program needn't handle non-finite values.
Results may differ from a plain program's by a relative error of at most 0.012.
The roundings to bfloat16 on the way count: a program that leaves them out, or rounds other values in their place, can miss the bound.
Values may be sent and summed in bfloat16 or wider, within the bound.
A program may use at most 64 MiB of HBM per device.

v0:
```python
import jax
import jax.numpy as jnp
from jax import lax
from jax.sharding import PartitionSpec as P


def local_prior(current, weights, offsets):
    picked = jnp.take(current, offsets, axis=3)
    return jnp.sum(picked * weights[None], axis=(1, 2))


def shards(ensemble, obs_weight, obs_value, obs_tile, obs_offset, obs_gain, localize):
    members, fields, levels, col_width = ensemble.shape
    tile_count = lax.axis_size("col")
    my_tile = lax.axis_index("col")
    batches, observed = obs_value.shape
    capacity = 4 * observed // tile_count
    current = ensemble
    for batch_index in range(batches):
        tile_ids = obs_tile[batch_index, :, 0]
        is_owned = tile_ids == my_tile
        partial_value = jnp.where(
            is_owned[None, :],
            local_prior(current, obs_weight[batch_index], obs_offset[batch_index]),
            0.0,
        )
        onehot = (tile_ids[:, None] == jnp.arange(tile_count, dtype=jnp.int32)[None, :]).astype(
            jnp.int32
        )
        slot_rank = jnp.sum(jnp.cumsum(onehot, axis=0) * onehot, axis=1) - 1
        slot_pick = (
            is_owned[:, None]
            & (slot_rank[:, None] == jnp.arange(capacity, dtype=jnp.int32)[None, :])
        ).astype(jnp.float32)
        packed = jnp.dot(partial_value, slot_pick, precision=lax.Precision.HIGHEST)
        packed = lax.psum(packed, "lev")
        gathered = lax.all_gather(packed, "col", axis=1, tiled=True)
        prior_ens = jnp.take(gathered, tile_ids * capacity + slot_rank, axis=1)
        prior_mean = jnp.mean(prior_ens, axis=0)
        prior_anom = prior_ens - prior_mean[None]
        variance = jnp.sum(prior_anom * prior_anom, axis=0) / (members - 1) + 1e-06
        innovation = (obs_value[batch_index][None] - prior_ens).astype(jnp.bfloat16)
        own_rows = lax.dot_general(
            innovation,
            obs_gain[batch_index],
            (((1,), (1,)), ((), ())),
            preferred_element_type=jnp.float32,
        ).astype(jnp.bfloat16)
        anom_short = prior_anom.astype(jnp.bfloat16)
        inv_scale = 1.0 / ((members - 1) * variance)
        state_anom = (
            (current - jnp.mean(current, axis=0)[None]).astype(jnp.bfloat16).reshape(members, -1)
        )
        covariance = lax.dot_general(
            anom_short, state_anom, (((0,), (0,)), ((), ())), preferred_element_type=jnp.float32
        )
        covariance = covariance.reshape(observed, fields * levels, col_width)
        coefficient = (
            (covariance * inv_scale[:, None, None] * localize[batch_index][:, None, :])
            .astype(jnp.bfloat16)
            .reshape(observed, -1)
        )
        change = jnp.dot(
            lax.all_gather(own_rows, "lev", axis=1, tiled=True),
            coefficient,
            preferred_element_type=jnp.float32,
        )
        current = current + change.reshape(current.shape)
    return current


def solution(mesh):
    in_specs = (
        P(None, None, "lev", "col"),
        P(None, None, "lev", None),
        P(),
        P(),
        P(),
        P(None, "lev", None),
        P(None, None, "col"),
    )
    out_specs = P(None, None, "lev", "col")
    return jax.shard_map(shards, mesh=mesh, in_specs=in_specs, out_specs=out_specs, check_vma=False)
```

profile of v0, /device:TPU:1, one launch (start us, length us, event | category | flops | bytes accessed | tf_op | source)
XLA Modules:
  0.0 714.2 jit_solution(5485141527000889267)
XLA Ops:
  8.2 9.0 %reduce-window.30 = s32[32,8,128]{2,1,0:T(8,128)S(1)} reduce-window(s32[32,8,128]{2,1,0:T(8,128)S(1)} %fusion.109, s32[]{:T(128)} %constant.62.clone.1), window={size=1x1x128 pad=0_0x0_0x127_0}, to_apply=%region_9.12 | reduce-window | flops 4161536 | bytes 262148 | tf_op jit(solution)/shard_map/reduce-window.2
  17.7 9.0 %reduce-window.26 = s32[32,8,128]{2,1,0:T(8,128)S(1)} reduce-window(s32[32,8,128]{2,1,0:T(8,128)S(1)} %fusion.108, s32[]{:T(128)} %constant.62.clone.1), window={size=1x1x128 pad=0_0x0_0x127_0}, to_apply=%region_1.3 | reduce-window | flops 4161536 | bytes 262148 | tf_op jit(solution)/shard_map/reduce-window
  30.6 10.0 %gather_fusion = f32[1024,80,4,2]{1,2,3,0:T(4,128)} fusion(f32[80,4,2,512]{0,1,3,2:T(4,128)S(1)} %copy.61, s32[1024]{0:T(1024)S(1)} %fusion.112), kind=kCustom, calls=%fused_computation.clone | custom fusion | bytes 5246976 | tf_op jit(solution)/shard_map/jit(_take)/gather | solution.py:8
  40.7 8.0 %fusion.3 = f32[80,1024]{0,1:T(8,128)S(1)} fusion(f32[1024,80,4,2]{1,2,3,0:T(4,128)} %gather_fusion, f32[4,2,1024]{0,1,2:T(2,128)S(1)} %copy.62, pred[1024]{0:T(1024)(128)(4,1)S(1)} %compare_and_fusion.7), kind=kLoop, calls=%fused_computation.19 | loop fusion | flops 1884160 | bytes 2982912 | tf_op jit(solution)/shard_map/reduce_sum | solution.py:9
  49.7 37.1 %psum.28 = f32[80,128]{1,0:T(8,128)} all-reduce(f32[80,128]{1,0:T(8,128)S(1)} %fusion.22), channel_id=1, replica_groups=mesh['col'=32,'lev'=8] {'lev'}, use_global_device_ids=true, to_apply=%region_4.6 | all-reduce | flops 10240 | bytes 81920 | tf_op jit(solution)/shard_map/psum | solution.py:36
  86.9 6.0 bitcast_convert_fusion
  103.0 52.9 %all-gather.5.cloned.1.call-done = f32[80,4096]{1,0:T(8,128)} async-done(((f32[80,128]{1,0:T(8,128)}), f32[80,4096]{1,0:T(8,128)}) %all-gather.5.cloned.1.call-update) | async-done | bytes 1310736 | tf_op jit(solution)/shard_map/all_gather | solution.py:37
  158.7 4.4 gather_fusion.1
  165.5 26.5 %all_gather.25 = bf16[80,1024]{1,0:T(8,128)(2,1)S(1)} all-gather(bf16[80,128]{1,0:T(8,128)(2,1)S(1)} %convolution_convert_fusion.3), channel_id=1, replica_groups=mesh['col'=32,'lev'=8] {'lev'}, dimensions={1}, use_global_device_ids=true | all-gather | bytes 184320 | tf_op jit(solution)/shard_map/all_gather | solution.py:64
  192.0 4.5 multiply_convert_fusion.3
  200.6 10.0 %gather_fusion.2 = f32[1024,80,4,2]{1,2,3,0:T(4,128)} fusion(f32[80,4,2,512]{0,1,3,2:T(4,128)S(1)} %copy.70, s32[1024]{0:T(1024)S(1)} %fusion.113), kind=kCustom, calls=%fused_computation.2.clone | custom fusion | bytes 5246976 | tf_op jit(solution)/shard_map/jit(_take)/gather | solution.py:8
  210.6 8.1 %fusion.2 = f32[80,1024]{0,1:T(8,128)S(1)} fusion(f32[1024,80,4,2]{1,2,3,0:T(4,128)} %gather_fusion.2, f32[4,2,1024]{0,1,2:T(2,128)} %copy.71, pred[1024]{0:T(1024)(128)(4,1)S(1)} %compare_and_fusion.5), kind=kLoop, calls=%fused_computation.17 | loop fusion | flops 1884160 | bytes 2982912 | tf_op jit(solution)/shard_map/reduce_sum | solution.py:9
  219.8 34.4 %psum.29 = f32[80,128]{1,0:T(8,128)} all-reduce(f32[80,128]{1,0:T(8,128)S(1)} %fusion.20), channel_id=1, replica_groups=mesh['col'=32,'lev'=8] {'lev'}, use_global_device_ids=true, to_apply=%region_12.15 | all-reduce | flops 10240 | bytes 81920 | tf_op jit(solution)/shard_map/psum | solution.py:36
  254.3 9.0 %reduce-window.36 = s32[32,8,128]{2,1,0:T(8,128)S(1)} reduce-window(s32[32,8,128]{2,1,0:T(8,128)S(1)} %fusion.111, s32[]{:T(128)} %constant.62.clone.1), window={size=1x1x128 pad=0_0x0_0x127_0}, to_apply=%region_25.28 | reduce-window | flops 4161536 | bytes 262148 | tf_op jit(solution)/shard_map/reduce-window.6
  263.7 9.0 %reduce-window.34 = s32[32,8,128]{2,1,0:T(8,128)S(1)} reduce-window(s32[32,8,128]{2,1,0:T(8,128)S(1)} %fusion.110, s32[]{:T(128)} %constant.62.clone.1), window={size=1x1x128 pad=0_0x0_0x127_0}, to_apply=%region_17.20 | reduce-window | flops 4161536 | bytes 262148 | tf_op jit(solution)/shard_map/reduce-window.4
  275.6 48.0 %all-gather.7.cloned.1.call-done = f32[80,4096]{1,0:T(8,128)} async-done(((f32[80,128]{1,0:T(8,128)}), f32[80,4096]{1,0:T(8,128)}) %all-gather.7.cloned.1.call-update) | async-done | bytes 1310736 | tf_op jit(solution)/shard_map/all_gather | solution.py:37
  334.1 26.1 %all_gather.27 = bf16[80,1024]{1,0:T(8,128)(2,1)S(1)} all-gather(bf16[80,128]{1,0:T(8,128)(2,1)S(1)} %convolution_convert_fusion.2), channel_id=1, replica_groups=mesh['col'=32,'lev'=8] {'lev'}, dimensions={1}, use_global_device_ids=true | all-gather | bytes 184320 | tf_op jit(solution)/shard_map/all_gather | solution.py:64
  360.2 4.5 multiply_convert_fusion.2
  369.3 11.7 %gather_fusion.4 = f32[1024,80,4,2]{1,2,3,0:T(4,128)} fusion(f32[80,4,2,512]{0,1,3,2:T(4,128)} %copy.79, s32[1024]{0:T(1024)S(1)} %fusion.114), kind=kCustom, calls=%fused_computation.3.clone | custom fusion | bytes 5246976 | tf_op jit(solution)/shard_map/jit(_take)/gather | solution.py:8
  381.0 8.0 %fusion.1 = f32[80,1024]{0,1:T(8,128)S(1)} fusion(f32[1024,80,4,2]{1,2,3,0:T(4,128)} %gather_fusion.4, f32[4,2,1024]{0,1,2:T(2,128)S(1)} %copy-done.2, pred[1024]{0:T(1024)(128)(4,1)S(1)} %compare_and_fusion.3), kind=kLoop, calls=%fused_computation.15 | loop fusion | flops 1884160 | bytes 2982912 | tf_op jit(solution)/shard_map/reduce_sum | solution.py:9
  390.0 34.4 %psum.30 = f32[80,128]{1,0:T(8,128)} all-reduce(f32[80,128]{1,0:T(8,128)S(1)} %fusion.18), channel_id=1, replica_groups=mesh['col'=32,'lev'=8] {'lev'}, use_global_device_ids=true, to_apply=%region_20.23 | all-reduce | flops 10240 | bytes 81920 | tf_op jit(solution)/shard_map/psum | solution.py:36
  430.1 64.1 %all-gather.9.cloned.1.call-done = f32[80,4096]{1,0:T(8,128)} async-done(((f32[80,128]{1,0:T(8,128)}), f32[80,4096]{1,0:T(8,128)}) %all-gather.9.cloned.1.call-update) | async-done | bytes 1310736 | tf_op jit(solution)/shard_map/all_gather | solution.py:37
  497.0 4.4 gather_fusion.5
  503.8 26.2 %all_gather.29 = bf16[80,1024]{1,0:T(8,128)(2,1)S(1)} all-gather(bf16[80,128]{1,0:T(8,128)(2,1)S(1)} %convolution_convert_fusion.1), channel_id=1, replica_groups=mesh['col'=32,'lev'=8] {'lev'}, dimensions={1}, use_global_device_ids=true | all-gather | bytes 184320 | tf_op jit(solution)/shard_map/all_gather | solution.py:64
  530.0 4.5 multiply_convert_fusion.1
  538.2 10.0 %gather_fusion.6 = f32[1024,80,4,2]{1,2,3,0:T(4,128)} fusion(f32[80,4,2,512]{0,1,3,2:T(4,128)S(1)} %copy.88, s32[1024]{0:T(1024)S(1)} %fusion.115), kind=kCustom, calls=%fused_computation.4.clone | custom fusion | bytes 5246976 | tf_op jit(solution)/shard_map/jit(_take)/gather | solution.py:8
  548.2 8.3 %fusion = f32[80,1024]{0,1:T(8,128)S(1)} fusion(f32[1024,80,4,2]{1,2,3,0:T(4,128)} %gather_fusion.6, f32[4,2,1024]{0,1,2:T(2,128)} %copy.89, pred[1024]{0:T(1024)(128)(4,1)S(1)} %compare_and_fusion.1), kind=kLoop, calls=%fused_computation.13 | loop fusion | flops 1884160 | bytes 2982912 | tf_op jit(solution)/shard_map/reduce_sum | solution.py:9
  557.5 34.4 %psum.31 = f32[80,128]{1,0:T(8,128)} all-reduce(f32[80,128]{1,0:T(8,128)S(1)} %fusion.16), channel_id=1, replica_groups=mesh['col'=32,'lev'=8] {'lev'}, use_global_device_ids=true, to_apply=%region_28.31 | all-reduce | flops 10240 | bytes 81920 | tf_op jit(solution)/shard_map/psum | solution.py:36
  596.0 65.3 %all-gather.11.cloned.1.call-done = f32[80,4096]{1,0:T(8,128)} async-done(((f32[80,128]{1,0:T(8,128)}), f32[80,4096]{1,0:T(8,128)}) %all-gather.11.cloned.1.call-update) | async-done | bytes 1310736 | tf_op jit(solution)/shard_map/all_gather | solution.py:37
  663.2 4.0 gather_fusion.7
  671.8 26.3 %all_gather.31 = bf16[80,1024]{1,0:T(8,128)(2,1)S(1)} all-gather(bf16[80,128]{1,0:T(8,128)(2,1)S(1)} %convolution_convert_fusion), channel_id=1, replica_groups=mesh['col'=32,'lev'=8] {'lev'}, dimensions={1}, use_global_device_ids=true | all-gather | bytes 184320 | tf_op jit(solution)/shard_map/all_gather | solution.py:64
  698.1 4.5 multiply_convert_fusion
  (130 shorter events, 77.3 us)
Async XLA Ops:
  6.5 23.4 %copy-start.3 = (f32[4,4,2,1024]{3,2,1,0:T(2,128)S(1)}, f32[4,4,2,1024]{3,2,1,0:T(2,128)}, u32[]{:S(2)}) copy-start(f32[4,4,2,1024]{3,2,1,0:T(2,128)} %param.12) | copy-start | bytes 393220
  6.5 149.4 %all-gather.5.cloned.1.call-start = ((), (), s32[]{:S(2)}) async-start(), calls=%async_computation | async-start | bytes 1351680 | tf_op jit(solution)/shard_map/all_gather | solution.py:37
  86.8 236.9 %all-gather.7.cloned.1.call-start = ((), (), s32[]{:S(2)}) async-start(), calls=%async_computation.1 | async-start | bytes 1351680 | tf_op jit(solution)/shard_map/all_gather | solution.py:37
  92.9 3.1 copy-start
  97.0 6.0 copy-start.4
  254.3 240.0 %all-gather.9.cloned.1.call-start = ((), (), s32[]{:S(2)}) async-start(), calls=%async_computation.2 | async-start | bytes 1351680 | tf_op jit(solution)/shard_map/all_gather | solution.py:37
  367.5 13.5 %copy-start.2 = (f32[4,2,1024]{0,1,2:T(2,128)S(1)}, f32[4,2,1024]{0,1,2:T(2,128)}, u32[]{:S(2)}) copy-start(f32[4,2,1024]{0,1,2:T(2,128)} %copy.80) | copy-start | bytes 98308
  424.5 236.9 %all-gather.11.cloned.1.call-start = ((), (), s32[]{:S(2)}) async-start(), calls=%async_computation.3 | async-start | bytes 1351680 | tf_op jit(solution)/shard_map/all_gather | solution.py:37
  548.2 43.8 %copy-start.1 = (f32[1024,512]{1,0:T(8,128)S(1)}, f32[1024,512]{1,0:T(8,128)}, u32[]{:S(2)}) copy-start(f32[1024,512]{1,0:T(8,128)} %get-tuple-element.6) | copy-start | bytes 6291460
Sparse Core Ops, SparseCore 0:
  86.9 68.9 all-gather.4
  254.4 69.2 all-gather.6
  424.6 69.5 all-gather.8
  592.1 69.2 all-gather.10
where the time goes:
time: 725 us; the launch traced here: 714 us
  blocking collectives  245 us (34%)
  waiting for transfers between devices  230 us (32%)
  local copies, waits for them, and re-layouts  99.8 us (14%)
  other arithmetic  84.5 us (12%)
  matrix products  39.8 us (5%)
  between operations  14.1 us (2%)
    all_gather x4, waiting for transfers between devices, shards(): gathered = lax.all_gather(packed, 'col', axis=1, tiled=True)  230 us
    psum x4, blocking collectives, shards(): packed = lax.psum(packed, 'lev')  140 us
    all_gather x4, blocking collectives, shards(): lax.all_gather(own_rows, 'lev', axis=1, tiled=True)  105 us
    gather x4, local copies, waits for them, and re-layouts, local_prior(): picked = jnp.take(current, offsets, axis=3)  41.8 us
    another operation x12, other arithmetic  36.6 us
    reduce_sum x4, other arithmetic, local_prior(): return jnp.sum(picked * weights[None], axis=(1, 2))  32.3 us
    dot_general x4, matrix products, shards(): lax.dot_general(anom_short, state_anom, (((0,), (0,)), ((), ())), preferr...  18 us
    gather x4, local copies, waits for them, and re-layouts, shards(): prior_ens = jnp.take(gathered, tile_ids * capacity + slot_rank, axis=1)  16.8 us
  transfers between devices with their start and end apart: 4, of which 4 were waited for; matrix products, arithmetic and copies ran while one was open for 7% of the time, Pallas kernels for 0%

commit v1 on v0

v1 whole, which is shorter than its diff:
```python
import jax
import jax.numpy as jnp
from jax import lax
from jax.experimental import pallas as pl
from jax.experimental.pallas import tpu as pltpu
from jax.sharding import PartitionSpec as P

F32, BF16, I32 = jnp.float32, jnp.bfloat16, jnp.int32
MESH = pl.DeviceIdType.MESH
MEMBERS = 80
PAD = 128
NB = 4
NOBS = 1024
NCOL, NLEV = 32, 8
FL = 8
WIDTH = 512


def iota(shape, axis):
    return lax.broadcasted_iota(I32, shape, axis)


def dot(a, b):
    return lax.dot_general(a, b, (((1,), (0,)), ((), ())), preferred_element_type=F32)


def dot_nt(a, b):
    return lax.dot_general(a, b, (((1,), (1,)), ((), ())), preferred_element_type=F32)


def parts(x, count):
    out = []
    for _ in range(count):
        piece = x.astype(BF16)
        out.append(piece)
        x = x - piece.astype(F32)
    return out


def wait_bytes(ref, sem):
    pltpu.make_async_copy(ref, ref, sem).wait()


def loop(count, body):
    lax.fori_loop(0, count, lambda k, c: (body(k), c)[1], 0)


def kernel(
    tile_ref, off_ref, val_ref, w_ref, ens_hbm, gain_hbm, loc_hbm, out_hbm,
    cur, gain, loc, oh, x, xt, xn, xa, rs, zs, zr, inn, an, inc, perm, gainp, lsel,
    aj, locs, dhi, dlo, sa, coef, gcol, wsl, cmat, ovs,
    in_sem, out_sem, rs_s, rs_r, ag_s, ag_r, z_s, z_r, wi_s, wi_r, wa_s, wa_r,
    fi_s, fi_r, fa_s, fa_r, ic_s, ic_r,
):
    col, lev = lax.axis_index("col"), lax.axis_index("lev")
    z, quad = col // 4, col % 4
    x_lo, core = quad // 2, quad % 2
    sibling = col + 1 - 2 * core
    spot = lev * 2 + x_lo
    rho = core * 16 + spot

    loads = [pltpu.make_async_copy(ens_hbm, cur, in_sem.at[0]),
             pltpu.make_async_copy(gain_hbm, gain, in_sem.at[1])]
    loads += [pltpu.make_async_copy(loc_hbm.at[b], loc.at[b], in_sem.at[2 + b]) for b in range(NB)]
    for load in loads:
        load.start()

    def chip(k):
        other = lax.rem(spot + k, 16)
        return z * 4 + (other % 2) * 2 + core, other // 2

    barrier = pltpu.get_barrier_semaphore()

    def greet_col(k):
        pl.semaphore_signal(barrier, inc=1, device_id={"col": lax.rem(col + k + 1, NCOL), "lev": lev}, device_id_type=MESH)

    def greet_chip(k):
        c, l = chip(k + 1)
        pl.semaphore_signal(barrier, inc=1, device_id={"col": c, "lev": l}, device_id_type=MESH)

    loop(NCOL - 1, greet_col)
    loop(15, greet_chip)

    tiles = tile_ref[...]
    member_of = jnp.concatenate(
        [jnp.where(tiles[b:b + 1, :] == iota((NCOL, NOBS), 0), 1.0, 0.0) for b in range(NB)], axis=0)
    member_b = member_of.astype(BF16)
    upper = jnp.where(iota((256, 256), 0) < iota((256, 256), 1), 1.0, 0.0).astype(BF16)
    ones = jnp.ones((256, 256), BF16)
    before, total = [], jnp.zeros((128, 256), F32)
    for k in range(4):
        block = member_b[:, 256 * k:256 * (k + 1)]
        before.append(dot(block, upper) + total)
        total = total + dot(block, ones)
    before = jnp.concatenate(before, axis=1)
    row, lane = iota((128, 128), 0), iota((128, 128), 1)
    lower = jnp.where((row // 32 == lane // 32) & (lane < row), 1.0, 0.0).astype(BF16)
    start = dot(lower, total[:, :128].astype(BF16))[:, :1]
    g_rows, code_rows = [], []
    for b in range(NB):
        mine = member_of[32 * b:32 * b + 32]
        begin = start[32 * b:32 * b + 32]
        g = jnp.sum(mine * (before[32 * b:32 * b + 32] + begin), axis=0, keepdims=True)
        g_rows.append(g)
        gi = g.astype(I32)
        first = jnp.sum(mine * begin, axis=0, keepdims=True).astype(I32)
        res = gi & 31
        rank = (gi >> 5) - ((first - res + 31) >> 5)
        slot = 16 * ((res >> 1) & 7) + 8 * (res & 1) + 4 * (res >> 4) + rank
        code_rows.append(jnp.where(tiles[b:b + 1, :] == col, slot, -1))
    gcol[...] = jnp.concatenate(g_rows + [jnp.zeros((4, NOBS), F32)], axis=0).T

    for b in range(NB):
        pick = jnp.where(code_rows[b] == iota((PAD, NOBS), 0), 1.0, 0.0).astype(BF16)
        off = off_ref[b:b + 1, :]
        head = jnp.concatenate(
            [(off >> 8).astype(F32), (off & 255).astype(F32), jnp.ones((1, NOBS), F32), jnp.zeros((5, NOBS), F32)], axis=0)
        wp = [p.astype(F32) for p in parts(w_ref[b], 3)]
        got = dot_nt(jnp.concatenate([head] + wp, axis=0).astype(BF16), pick)
        column = got[0:1] * 256.0 + got[1:2] + (got[2:3] - 1.0) * 10000.0
        wsl[:, 128 * b:128 * b + 128] = got[8:16] + got[16:24] + got[24:32]
        oh[:, 128 * b:128 * b + 128] = jnp.where(
            iota((WIDTH, PAD), 0) == column.astype(I32), 1.0, 0.0).astype(BF16)

    x[...] = jnp.zeros_like(x)
    loads[0].wait()

    def project(fl):
        got = dot(jnp.concatenate(parts(cur[fl], 3), axis=0), oh[...])
        x[0:MEMBERS, :] += (got[0:80] + got[80:160] + got[160:240]) * wsl[pl.ds(fl, 1), :]

    loop(FL, project)
    for b in range(NB):
        xt[b] = x[:, 128 * b:128 * b + 128].T.reshape(NLEV, 16, PAD)

    pl.semaphore_wait(barrier, NCOL - 1 + 15)

    def lev_peer(k):
        return lax.rem(lev + k + 1, NLEV)

    def send_first(k):
        to = lev_peer(k)
        pltpu.make_async_remote_copy(
            src_ref=xt.at[0, to], dst_ref=rs.at[lev, 0], send_sem=rs_s.at[0], recv_sem=rs_r.at[0],
            device_id={"col": col, "lev": to}, device_id_type=MESH).start()

    def send_rest(k):
        to = lev_peer(k)
        pltpu.make_async_remote_copy(
            src_ref=xt.at[pl.ds(1, 3), to], dst_ref=rs.at[lev, pl.ds(1, 3)], send_sem=rs_s.at[1], recv_sem=rs_r.at[1],
            device_id={"col": col, "lev": to}, device_id_type=MESH).start()

    loop(NLEV - 1, send_first)
    loop(NLEV - 1, send_rest)

    def place(b):
        want = ((iota((256, NOBS), 1) & 31) * 32 + (iota((256, NOBS), 1) >> 5)).astype(F32)

        def rows(k):
            at = pl.ds(pl.multiple_of(k * 256, 256), 256)
            perm[b % 2, at, :] = jnp.where(gcol[at, b:b + 1] == want, 1.0, 0.0).astype(BF16)

        loop(4, rows)
        gainp[b % 2] = dot(gain[b], perm[b % 2]).astype(BF16)

    def select(b):
        if b == NB - 1:
            return
        if b == 0:
            for load in loads[2:]:
                load.wait()
        wide = 128 * (NB - 1 - b)

        def rows(k):
            at = pl.ds(pl.multiple_of(k * 256, 256), 256)
            lsel[at, 0:wide] = dot(loc[b, at, :], oh[:, 128 * (b + 1):])

        loop(4, rows)

    def anomaly(fl):
        block = cur[fl]
        sa[fl, 0:MEMBERS, :] = (block - jnp.mean(block, axis=0, keepdims=True)).astype(BF16)

    def send_z(b):
        for k in range(4):
            zs[b, k] = xn[b, lev, 4 * k:4 * k + 4, :]
        zr[b, col] = zs[b, quad]

        def one(k):
            to = lax.rem(col + k + 1, NCOL)
            pltpu.make_async_remote_copy(
                src_ref=zs.at[b, to % 4], dst_ref=zr.at[b, col], send_sem=z_s.at[b], recv_sem=z_r.at[b],
                device_id={"col": to, "lev": lev}, device_id_type=MESH).start()

        loop(NCOL - 1, one)

    counts = dot_nt(jnp.ones((8, NOBS), BF16), member_b)
    own_batch = iota((8, 128), 1) // 32 == iota((8, 128), 0)
    counts = jnp.where(own_batch, counts, 0.0).astype(BF16)
    tile_row, tile_lane = iota((128, 128), 0) % 32, iota((128, 128), 1) // 4
    begins = dot(counts, jnp.where(tile_row < tile_lane, 1.0, 0.0).astype(BF16)).astype(I32)
    ends = dot(counts, jnp.where(tile_row <= tile_lane, 1.0, 0.0).astype(BF16)).astype(I32)
    q = iota((32, 128), 0)
    for b in range(NB):
        want = (iota((32, 128), 1) & 3) + ((begins[b:b + 1] - rho + 31) >> 5)
        cmat[b] = jnp.where((q == want) & (32 * q + rho < ends[b:b + 1]), 1.0, 0.0).astype(BF16)
        here = g_rows[b].astype(I32) == 32 * iota((32, NOBS), 0) + rho
        ovs[b] = jnp.broadcast_to(jnp.sum(jnp.where(here, val_ref[b:b + 1, :], 0.0), axis=1, keepdims=True), (32, PAD))

    sa[...] = jnp.zeros_like(sa)
    loads[1].wait()
    place(0)

    wait_bytes(rs.at[pl.ds(0, 7), 0], rs_r.at[0])
    rs[lev, 0] = xt[0, lev]
    xn[0, lev] = jnp.sum(rs[:, 0], axis=0)
    send_z(0)

    wait_bytes(rs.at[pl.ds(0, 7), pl.ds(1, 3)], rs_r.at[1])
    for b in range(1, NB):
        rs[lev, b] = xt[b, lev]
        xa[b - 1, lev] = jnp.sum(rs[:, b], axis=0)

    def send_xa(k):
        to = lev_peer(k)
        pltpu.make_async_remote_copy(
            src_ref=xa.at[:, lev], dst_ref=xa.at[:, lev], send_sem=ag_s, recv_sem=ag_r,
            device_id={"col": col, "lev": to}, device_id_type=MESH).start()

    loop(NLEV - 1, send_xa)
    select(0)
    loop(FL, anomaly)

    lane_of = iota((32, PAD), 1)
    in_members = lane_of < MEMBERS

    def spread(buf, b, s_sem, r_sem):
        own = buf.at[b, pl.ds(pl.multiple_of(rho * 32, 32), 32)]

        def one(k):
            c, l = chip(k + 1)
            pltpu.make_async_remote_copy(
                src_ref=own, dst_ref=own, send_sem=s_sem.at[b], recv_sem=r_sem.at[b],
                device_id={"col": c, "lev": l}, device_id_type=MESH).start()

        loop(15, one)

    def forward(buf, b, r_sem, fs_sem, fr_sem):
        wait_bytes(buf.at[b, pl.ds(0, 480)], r_sem.at[b])
        half = buf.at[b, pl.ds(pl.multiple_of(core * 512, 512), 512)]
        pltpu.make_async_remote_copy(
            src_ref=half, dst_ref=half, send_sem=fs_sem.at[b], recv_sem=fr_sem.at[b],
            device_id={"col": sibling, "lev": lev}, device_id_type=MESH).start()

    def cov(b, fl):
        for h in range(2):
            at = slice(256 * h, 256 * h + 256)
            got = dot(aj[...], sa[fl, :, at]) * locs[:, at]
            coef[fl, :, at] = got.astype(BF16)

    def change(b, fl):
        cur[fl] += dot(inc[b], coef[fl])

    def out_copy(fl):
        return pltpu.make_async_copy(cur.at[fl], out_hbm.at[fl], out_sem)

    for b in range(NB):
        if b > 0:
            loop(FL, lambda fl: change(b - 1, fl))
        wait_bytes(zr.at[b, pl.ds(0, NCOL - 1)], z_r.at[b])
        got = zr[b].reshape(128, PAD)
        hi, lo = parts(got, 2)
        prior = dot(cmat[b], hi) + dot(cmat[b], lo)
        mean = jnp.sum(prior, axis=1, keepdims=True) * (1.0 / MEMBERS)
        anom = jnp.where(in_members, prior - mean, 0.0)
        variance = jnp.sum(anom * anom, axis=1, keepdims=True) / (MEMBERS - 1) + 1e-6
        scale = parts(1.0 / ((MEMBERS - 1) * variance), 3)
        mine = pl.ds(pl.multiple_of(rho * 32, 32), 32)
        inn[b, mine, :] = jnp.where(in_members, ovs[b] - prior, 0.0).astype(BF16)
        spread(inn, b, wi_s, wi_r)
        for k in range(3):
            anom = jnp.where(lane_of == MEMBERS + k, scale[k].astype(F32), anom)
        an[b, mine, :] = anom.astype(BF16)
        spread(an, b, wa_s, wa_r)
        if b == 0:
            wait_bytes(xa.at[:, pl.ds(0, 7)], ag_r)
            for k in range(1, NB):
                x[:, 128 * k:128 * k + 128] = xa[k - 1].reshape(128, PAD).T
        else:
            loop(FL, anomaly)
        forward(inn, b, wi_r, fi_s, fi_r)
        forward(an, b, wa_r, fa_s, fa_r)
        if b + 1 < NB:
            place(b + 1)
        wait_bytes(inn.at[b, pl.ds(0, 512)], fi_r.at[b])
        rows = dot(gainp[b % 2], inn[b])
        own = pl.ds(pl.multiple_of(lev * 128, 128), 128)
        inc[b, :, own] = rows.T[0:MEMBERS].astype(BF16)

        def send_inc(k):
            piece = inc.at[b, :, own]
            pltpu.make_async_remote_copy(
                src_ref=piece, dst_ref=piece, send_sem=ic_s.at[b], recv_sem=ic_r.at[b],
                device_id={"col": col, "lev": lev_peer(k)}, device_id_type=MESH).start()

        loop(NLEV - 1, send_inc)
        wait_bytes(an.at[b, pl.ds(0, 512)], fa_r.at[b])
        wide = 128 * (NB - 1 - b)
        if b + 1 < NB:
            future = x[:, 128 * (b + 1):]
            keep = iota((PAD, wide), 0) < MEMBERS
            future = jnp.where(keep, future - jnp.sum(future, axis=0, keepdims=True) * (1.0 / MEMBERS), 0.0)
            xh, xl = parts(future, 2)

        def unpack(k):
            at = pl.ds(pl.multiple_of(k * 256, 256), 256)
            got = dot(perm[b % 2, at, :], an[b])
            scale_col = got[:, 80:81] + got[:, 81:82] + got[:, 82:83]
            short = got.astype(BF16)
            aj[at, :] = short
            locs[at, :] = loc[b, at, :].astype(F32) * scale_col
            if b + 1 < NB:
                d = (dot(short, xh) + dot(short, xl)) * (lsel[at, 0:wide] * scale_col)
                high, low = parts(d, 2)
                dhi[at, 0:wide] = high
                dlo[at, 0:wide] = low

        loop(4, unpack)
        if b + 1 < NB:
            select(b + 1)
        loop(FL, lambda fl: cov(b, fl))
        wait_bytes(inc.at[b, :, pl.ds(0, 896)], ic_r.at[b])
        if b + 1 < NB:
            nxt = slice(128 * (b + 1), 128 * (b + 2))
            fresh = x[0:MEMBERS, nxt] + dot(inc[b], dhi[:, 0:128]) + dot(inc[b], dlo[:, 0:128])
            x[0:MEMBERS, nxt] = fresh
            xn[b + 1] = x[:, nxt].T.reshape(NLEV, 16, PAD)
            send_z(b + 1)
        if b + 2 < NB:
            later = slice(128 * (b + 2), 128 * NB)
            x[0:MEMBERS, later] += dot(inc[b], dhi[:, 128:wide]) + dot(inc[b], dlo[:, 128:wide])

    def finish(fl):
        change(NB - 1, fl)
        out_copy(fl).start()

    loop(FL, finish)
    wait_bytes(cur, out_sem)
    wait_bytes(rs.at[pl.ds(0, 7), 0], rs_s.at[0])
    wait_bytes(rs.at[pl.ds(0, 7), pl.ds(1, 3)], rs_s.at[1])
    wait_bytes(xa.at[:, pl.ds(0, 7)], ag_s)
    for b in range(NB):
        wait_bytes(zr.at[b, pl.ds(0, NCOL - 1)], z_s.at[b])
        wait_bytes(inn.at[b, pl.ds(0, 480)], wi_s.at[b])
        wait_bytes(an.at[b, pl.ds(0, 480)], wa_s.at[b])
        wait_bytes(inn.at[b, pl.ds(0, 512)], fi_s.at[b])
        wait_bytes(an.at[b, pl.ds(0, 512)], fa_s.at[b])
        wait_bytes(inc.at[b, :, pl.ds(0, 896)], ic_s.at[b])


def shards(ensemble, obs_weight, obs_value, obs_tile, obs_offset, obs_gain, localize):
    state = jnp.transpose(ensemble, (1, 2, 0, 3)).reshape(FL, MEMBERS, WIDTH)
    vmem, hbm = pl.BlockSpec(memory_space=pltpu.VMEM), pl.BlockSpec(memory_space=pl.ANY)
    dma = pltpu.SemaphoreType.DMA
    out = pl.pallas_call(
        kernel,
        out_shape=jax.ShapeDtypeStruct((FL, MEMBERS, WIDTH), F32),
        in_specs=[vmem] * 4 + [hbm] * 3,
        out_specs=hbm,
        scratch_shapes=[
            pltpu.VMEM((FL, MEMBERS, WIDTH), F32),
            pltpu.VMEM((NB, 128, NOBS), BF16),
            pltpu.VMEM((NB, NOBS, WIDTH), BF16),
            pltpu.VMEM((WIDTH, NB * 128), BF16),
            pltpu.VMEM((PAD, NB * 128), F32),
            pltpu.VMEM((NB, NLEV, 16, PAD), F32),
            pltpu.VMEM((NB, NLEV, 16, PAD), F32),
            pltpu.VMEM((NB - 1, NLEV, 16, PAD), F32),
            pltpu.VMEM((NLEV, NB, 16, PAD), F32),
            pltpu.VMEM((NB, 4, 4, PAD), F32),
            pltpu.VMEM((NB, NCOL, 4, PAD), F32),
            pltpu.VMEM((NB, NOBS, PAD), BF16),
            pltpu.VMEM((NB, NOBS, PAD), BF16),
            pltpu.VMEM((NB, MEMBERS, NOBS), BF16),
            pltpu.VMEM((2, NOBS, NOBS), BF16),
            pltpu.VMEM((2, 128, NOBS), BF16),
            pltpu.VMEM((NOBS, 384), F32),
            pltpu.VMEM((NOBS, PAD), BF16),
            pltpu.VMEM((NOBS, WIDTH), F32),
            pltpu.VMEM((NOBS, 384), BF16),
            pltpu.VMEM((NOBS, 384), BF16),
            pltpu.VMEM((FL, PAD, WIDTH), BF16),
            pltpu.VMEM((FL, NOBS, WIDTH), BF16),
            pltpu.VMEM((NOBS, 8), F32),
            pltpu.VMEM((8, NB * 128), F32),
            pltpu.VMEM((NB, 32, 128), BF16),
            pltpu.VMEM((NB, 32, PAD), F32),
            dma((6,)), dma, dma((2,)), dma((2,)), dma, dma,
            dma((NB,)), dma((NB,)), dma((NB,)), dma((NB,)), dma((NB,)), dma((NB,)),
            dma((NB,)), dma((NB,)), dma((NB,)), dma((NB,)), dma((NB,)), dma((NB,)),
        ],
        compiler_params=pltpu.CompilerParams(
            collective_id=0, has_side_effects=True, vmem_limit_bytes=56 * 1024 * 1024),
        cost_estimate=pl.CostEstimate(flops=8 * 335544320, bytes_accessed=8 * 1024 * 1024, transcendentals=0),
    )(
        obs_tile[:, :, 0], obs_offset, obs_value, obs_weight.reshape(NB, FL, NOBS), state, obs_gain, localize,
    )
    return jnp.transpose(out.reshape(4, 2, MEMBERS, WIDTH), (2, 0, 1, 3))


def solution(mesh):
    in_specs = (
        P(None, None, "lev", "col"),
        P(None, None, "lev", None),
        P(),
        P(),
        P(),
        P(None, "lev", None),
        P(None, None, "col"),
    )
    out_specs = P(None, None, "lev", "col")
    return jax.shard_map(shards, mesh=mesh, in_specs=in_specs, out_specs=out_specs, check_vma=False)
```

time: 725 us -> 110 us (0.15); the launches traced: 714 us -> 110 us
  blocking collectives: 245 us -> 0 us
  waiting for transfers between devices: 230 us -> 0 us
  Pallas kernels: 0 us -> 100 us
  local copies, waits for them, and re-layouts: 99.8 us -> 9.48 us
  other arithmetic: 84.5 us -> 0 us
  matrix products: 39.8 us -> 0 us
  between operations: 14.1 us -> 0.01 us
    all_gather x4 -> x0, waiting for transfers between devices: 230 us -> none  [shards(): gathered = lax.all_gather(packed, 'col', axis=1, tiled=True)]
    psum x4 -> x0, blocking collectives: 140 us -> none  [shards(): packed = lax.psum(packed, 'lev')]
    all_gather x4 -> x0, blocking collectives: 105 us -> none  [shards(): lax.all_gather(own_rows, 'lev', axis=1, tiled=True)]
    pallas_call x0 -> x1, Pallas kernels: none -> 100 us  [shards(): pl.pallas_call(kernel, out_shape=jax.ShapeDtypeStruct((FL, MEMBERS, WIDTH...]
    gather x8 -> x0, local copies, waits for them, and re-layouts: 58.6 us -> none  [the longest x4 41.8 us: local_prior(): picked = jnp.take(current, offsets, axis=3)]
    reduce_sum x17 -> x0, other arithmetic: 40.6 us -> none  [the longest x4 32.3 us: local_prior(): return jnp.sum(picked * weights[None], axis=(1, 2))]
    dot_general x16 -> x0, matrix products: 39.8 us -> none  [the longest x4 18 us: shards(): lax.dot_general(anom_short, state_anom, (((0,), (0,)), ((), ())), preferr...]
    another operation x12 -> x0, other arithmetic: 36.6 us -> none
  transfers between devices with their start and end apart: 4 -> 0, of which waited for: 4 -> 0; matrix products, arithmetic and copies ran while one was open for 7% -> 0% of each run, Pallas kernels for 0% -> 0%
where the time goes in v1:
time: 110 us
  Pallas kernels  100 us (91%)
  local copies, waits for them, and re-layouts  9.48 us (9%)
    pallas_call x1, Pallas kernels, shards(): pl.pallas_call(kernel, out_shape=jax.ShapeDtypeStruct((FL, MEMBERS, WIDTH...  100 us
    reshape x1, local copies, waits for them, and re-layouts, shards(): return jnp.transpose(out.reshape(4, 2, MEMBERS, WIDTH), (2, 0, 1, 3))  3.38 us
    transpose x1, local copies, waits for them, and re-layouts, shards(): state = jnp.transpose(ensemble, (1, 2, 0, 3)).reshape(FL, MEMBERS, WIDTH)  3.13 us

profile of v1, /device:TPU:1, one launch (start us, length us, event | category | flops | bytes accessed | tf_op | source)
XLA Modules:
  0.0 110.0 jit_solution(7332205352866362041)
XLA Ops:
  0.0 1.3 %copy.14 = s32[4,1024,1]{1,0,2:T(4,128)} copy(s32[4,1024,1]{1,2,0:T(1,128)} %param.10) | data formatting | bytes 32768
  1.3 1.6 %reshape.9.w_ref = f32[4,8,1024]{2,1,0:T(8,128)} reshape(f32[4,4,2,1024]{3,2,1,0:T(2,128)} %param.8) | data formatting | bytes 262144 | tf_op jit(solution)/shard_map/reshape | solution.py:406
  3.0 3.1 %copy.8 = f32[4,2,80,512]{3,2,1,0:T(8,128)} copy(f32[4,2,80,512]{3,1,0,2:T(2,128)} %bitcast.9) | data formatting | bytes 2621440 | tf_op jit(solution)/shard_map/transpose | solution.py:362
  6.1 100.5 %shard_map.73 = f32[8,80,512]{2,1,0:T(8,128)} custom-call(s32[4,1024]{1,0:T(4,128)} %bitcast.12, s32[4,1024]{1,0:T(4,128)} %off_ref.1, f32[4,1024]{1,0:T(4,128)} %val_ref.1, f32[4,8,1024]{2,1,0:T(8,128)} %reshape.9.w_ref, f32[8,80,512]{2,1,0:T(8,128)} %bitcast.11, bf16[4,128,1024]{2,1,0:T(8,128)(2,1)} %gain_hbm.1, bf16[4,1024,512]{2,1,0:T(8,128)(2,1)} %loc_hbm.1), custom_call_target="tpu_custom_call" | custom-call | flops 2684354560 | bytes 8388608 | tf_op jit(solution)/shard_map/pallas_call | solution.py:365
  106.6 3.4 %copy.13 = f32[4,2,80,512]{3,1,0,2:T(2,128)} copy(f32[4,2,80,512]{3,2,1,0:T(8,128)} %bitcast.10) | data formatting | bytes 2621440 | tf_op jit(solution)/shard_map/reshape | solution.py:408

commit v2 on v1

v2 whole, which is shorter than its diff:
```python
import jax
import jax.numpy as jnp
from jax import lax
from jax.experimental import pallas as pl
from jax.experimental.pallas import tpu as pltpu
from jax.sharding import PartitionSpec as P

F32, BF16, I32 = jnp.float32, jnp.bfloat16, jnp.int32
MESH = pl.DeviceIdType.MESH
MEMBERS = 80
PAD = 128
NB = 4
NOBS = 1024
NCOL, NLEV = 32, 8
FL = 8
WIDTH = 512


def iota(shape, axis):
    return lax.broadcasted_iota(I32, shape, axis)


def dot(a, b):
    return lax.dot_general(a, b, (((1,), (0,)), ((), ())), preferred_element_type=F32)


def dot_nt(a, b):
    return lax.dot_general(a, b, (((1,), (1,)), ((), ())), preferred_element_type=F32)


def parts(x, count):
    out = []
    for _ in range(count):
        piece = x.astype(BF16)
        out.append(piece)
        x = x - piece.astype(F32)
    return out


def wait_bytes(ref, sem):
    pltpu.make_async_copy(ref, ref, sem).wait()


def push(src, dst, s_sem, r_sem, col, lev):
    pltpu.make_async_remote_copy(
        src_ref=src, dst_ref=dst, send_sem=s_sem, recv_sem=r_sem,
        device_id={"col": col, "lev": lev}, device_id_type=MESH).start()


def loop(count, body):
    lax.fori_loop(0, count, lambda k, c: (body(k), c)[1], 0)


def kernel(
    tile_ref, off_ref, val_ref, w_ref, ens_hbm, gain_hbm, loc_hbm, out_hbm,
    raw, cur, gain, loc, oh, x, xt, got_t, own, rs, zs, zr, ls, lsend, lrecv, later, inn, an, inc, perm, gainp,
    aj, locs, dt, sa, coef, gcol, wsl, cmat, cbig, ovs,
    in_sem, out_sem, rs_s, rs_r, z_s, z_r, l_s, l_r, wi_s, wi_r, wa_s, wa_r,
    fi_s, fi_r, fa_s, fa_r, ic_s, ic_r,
):
    col, lev = lax.axis_index("col"), lax.axis_index("lev")
    z, quad = col // 4, col % 4
    x_lo, core = quad // 2, quad % 2
    sibling = col + 1 - 2 * core
    spot = lev * 2 + x_lo
    rho = core * 16 + spot

    loads = [pltpu.make_async_copy(ens_hbm, raw, in_sem.at[0]),
             pltpu.make_async_copy(gain_hbm, gain, in_sem.at[1])]
    loads += [pltpu.make_async_copy(loc_hbm.at[b], loc.at[b], in_sem.at[2 + b]) for b in range(NB)]
    for load in loads:
        load.start()

    def chip(k):
        other = lax.rem(spot + k, 16)
        return z * 4 + (other % 2) * 2 + core, other // 2

    barrier = pltpu.get_barrier_semaphore()

    def greet_col(k):
        pl.semaphore_signal(barrier, inc=1, device_id={"col": lax.rem(col + k + 1, NCOL), "lev": lev}, device_id_type=MESH)

    def greet_chip(k):
        c, l = chip(k + 1)
        pl.semaphore_signal(barrier, inc=1, device_id={"col": c, "lev": l}, device_id_type=MESH)

    loop(NCOL - 1, greet_col)
    loop(15, greet_chip)

    tiles = [tile_ref[b] for b in range(NB)]
    member_of = jnp.concatenate(
        [jnp.where(tiles[b] == iota((NCOL, NOBS), 0), 1.0, 0.0) for b in range(NB)], axis=0)
    member_b = member_of.astype(BF16)
    upper = jnp.where(iota((256, 256), 0) < iota((256, 256), 1), 1.0, 0.0).astype(BF16)
    ones = jnp.ones((256, 256), BF16)
    before, total = [], jnp.zeros((128, 256), F32)
    for k in range(4):
        block = member_b[:, 256 * k:256 * (k + 1)]
        before.append(dot(block, upper) + total)
        total = total + dot(block, ones)
    before = jnp.concatenate(before, axis=1)
    row, lane = iota((128, 128), 0), iota((128, 128), 1)
    lower = jnp.where((row // 32 == lane // 32) & (lane < row), 1.0, 0.0).astype(BF16)
    start = dot(lower, total[:, :128].astype(BF16))[:, :1]
    g_rows, code_rows = [], []
    for b in range(NB):
        mine = member_of[32 * b:32 * b + 32]
        begin = start[32 * b:32 * b + 32]
        g = jnp.sum(mine * (before[32 * b:32 * b + 32] + begin), axis=0, keepdims=True)
        g_rows.append(g)
        gi = g.astype(I32)
        first = jnp.sum(mine * begin, axis=0, keepdims=True).astype(I32)
        res = gi & 31
        rank = (gi >> 5) - ((first - res + 31) >> 5)
        slot = 16 * ((res >> 1) & 7) + 8 * (res & 1) + 4 * (res >> 4) + rank
        code_rows.append(jnp.where(tiles[b] == col, slot, -1))

    for b in range(NB):
        pick = jnp.where(code_rows[b] == iota((PAD, NOBS), 0), 1.0, 0.0).astype(BF16)
        off = off_ref[b:b + 1, :]
        head = jnp.concatenate(
            [(off >> 8).astype(F32), (off & 255).astype(F32), jnp.ones((1, NOBS), F32), jnp.zeros((5, NOBS), F32)], axis=0)
        weights = jnp.concatenate(
            [jnp.concatenate([w_ref[pl.ds(64 * b + 2 * c + l, 4, stride=16), :] for l in range(2)], axis=0)
             for c in range(8)], axis=1)
        wp = [p.astype(F32) for p in parts(weights, 3)]
        got = dot_nt(jnp.concatenate([head] + wp, axis=0).astype(BF16), pick)
        column = got[0:1] * 256.0 + got[1:2] + (got[2:3] - 1.0) * 10000.0
        wsl[:, 128 * b:128 * b + 128] = got[8:16] + got[16:24] + got[24:32]
        oh[:, 128 * b:128 * b + 128] = jnp.where(
            iota((WIDTH, PAD), 0) == column.astype(I32), 1.0, 0.0).astype(BF16)
        got_t[b] = jnp.broadcast_to(column, (8, PAD)).T

    x[...] = jnp.zeros_like(x)
    loads[0].wait()

    def rows_of(fl, c):
        return pl.ds((fl % 4) * 8 + fl // 4 + 2 * c, MEMBERS, stride=32)

    def project(fl):
        block = jnp.concatenate([raw[rows_of(fl, c), :] for c in range(4)], axis=1)
        cur[fl] = block
        sa[fl, 0:MEMBERS, :] = (block - jnp.mean(block, axis=0, keepdims=True)).astype(BF16)
        got = dot(jnp.concatenate(parts(block, 3), axis=0), oh[...])
        x[0:MEMBERS, :] += (got[0:80] + got[80:160] + got[160:240]) * wsl[pl.ds(fl, 1), :]

    sa[...] = jnp.zeros_like(sa)
    loop(FL, project)
    for b in range(NB):
        xt[b] = x[:, 128 * b:128 * b + 128].T.reshape(NLEV, 16, PAD)

    pl.semaphore_wait(barrier, NCOL - 1 + 15)

    def lev_peer(k):
        return lax.rem(lev + k + 1, NLEV)

    def send_first(k):
        to = lev_peer(k)
        push(xt.at[0, to], rs.at[lev, 0], rs_s.at[0], rs_r.at[0], col, to)

    def send_rest(k):
        to = lev_peer(k)
        push(xt.at[pl.ds(1, 3), to], rs.at[lev, pl.ds(1, 3)], rs_s.at[1], rs_r.at[1], col, to)

    loop(NLEV - 1, send_first)
    loop(NLEV - 1, send_rest)

    gcol[...] = jnp.concatenate(g_rows + [jnp.zeros((4, NOBS), F32)], axis=0).T
    inc[...] = jnp.zeros_like(inc)

    def place(b):
        want = ((iota((256, NOBS), 1) & 31) * 32 + (iota((256, NOBS), 1) >> 5)).astype(F32)

        def rows(k):
            at = pl.ds(pl.multiple_of(k * 256, 256), 256)
            perm[b % 2, at, :] = jnp.where(gcol[at, b:b + 1] == want, 1.0, 0.0).astype(BF16)

        loop(4, rows)
        gainp[b % 2] = dot(gain[b], perm[b % 2]).astype(BF16)

    loads[1].wait()
    place(0)

    mine16 = pl.ds(pl.multiple_of(lev * 16, 16), 16)
    here = [jnp.where(got_t[b, mine16, 0:1].astype(I32) == iota((16, WIDTH), 1), 1.0, 0.0) for b in range(1, NB)]
    for b in range(NB - 1):
        loads[2 + b].wait()
        got = dot_nt(jnp.concatenate(here[b:], axis=0).astype(BF16), loc[b])
        if b + 2 < NB:
            later[b, 0:16 * (NB - 2 - b), :] = got[16:]
        for k in range(4):
            for c in range(8):
                ls[k, c] = got[4 * k:4 * k + 4, 128 * c:128 * c + 128]
        lsend[b] = ls[...].reshape(4, 32, PAD).astype(BF16)

    counts = dot_nt(jnp.ones((8, NOBS), BF16), member_b)
    counts = jnp.where(iota((8, 128), 1) // 32 == iota((8, 128), 0), counts, 0.0).astype(BF16)

    def edges(lanes, per_tile):
        at, of = iota((128, lanes), 0) % 32, iota((128, lanes), 1) // per_tile
        low = dot(counts, jnp.where(at < of, 1.0, 0.0).astype(BF16)).astype(I32)
        high = dot(counts, jnp.where(at <= of, 1.0, 0.0).astype(BF16)).astype(I32)
        return low, high

    low, high = edges(128, 4)
    q = iota((32, 128), 0)
    for b in range(NB):
        want = (iota((32, 128), 1) & 3) + ((low[b:b + 1] - rho + 31) >> 5)
        cmat[b] = jnp.where((q == want) & (32 * q + rho < high[b:b + 1]), 1.0, 0.0).astype(BF16)
        is_here = g_rows[b].astype(I32) == 32 * iota((32, NOBS), 0) + rho
        ovs[b] = jnp.broadcast_to(jnp.sum(jnp.where(is_here, val_ref[b:b + 1, :], 0.0), axis=1, keepdims=True), (32, PAD))

    def send_z(b):
        zr[b, col] = zs[b, quad]

        def one(k):
            to = lax.rem(col + k + 1, NCOL)
            push(zs.at[b, to % 4], zr.at[b, col], z_s.at[b], z_r.at[b], to, lev)

        loop(NCOL - 1, one)

    def send_l(b):
        lrecv[b, col] = lsend[b, quad]

        def one(k):
            to = lax.rem(col + k + 1, NCOL)
            push(lsend.at[b, to % 4], lrecv.at[b, col], l_s.at[b], l_r.at[b], to, lev)

        loop(NCOL - 1, one)

    wait_bytes(rs.at[pl.ds(0, 7), 0], rs_r.at[0])
    rs[lev, 0] = xt[0, lev]
    first = jnp.sum(rs[:, 0], axis=0)
    for k in range(4):
        zs[0, k] = first[4 * k:4 * k + 4]
    send_z(0)
    wait_bytes(rs.at[pl.ds(0, 7), pl.ds(1, 3)], rs_r.at[1])
    for b in range(1, NB):
        rs[lev, b] = xt[b, lev]
        own[b] = jnp.sum(rs[:, b], axis=0)
    for k in range(4):
        zs[1, k] = own[1, 4 * k:4 * k + 4]
    send_z(1)
    send_l(0)

    low, high = edges(NOBS, 32)
    row_q, row_c = iota((256, NOBS), 0) % 32, iota((256, NOBS), 0) // 32
    lane_c, lane_r = (iota((256, NOBS), 1) >> 2) & 7, iota((256, NOBS), 1) & 3
    for b in range(1, NB):
        want = lane_r + ((low[b:b + 1] - rho + 31) >> 5)
        hit = (row_q == want) & (row_c == lane_c) & (32 * row_q + rho < high[b:b + 1])
        cbig[b - 1] = jnp.where(hit, 1.0, 0.0).astype(BF16)

    lane_of = iota((32, PAD), 1)
    in_members = lane_of < MEMBERS

    def spread(buf, b, s_sem, r_sem):
        piece = buf.at[b, pl.ds(pl.multiple_of(rho * 32, 32), 32)]

        def one(k):
            c, l = chip(k + 1)
            push(piece, piece, s_sem.at[b], r_sem.at[b], c, l)

        loop(15, one)

    def forward(buf, b, r_sem, fs_sem, fr_sem):
        wait_bytes(buf.at[b, pl.ds(0, 480)], r_sem.at[b])
        half = buf.at[b, pl.ds(pl.multiple_of(core * 512, 512), 512)]
        push(half, half, fs_sem.at[b], fr_sem.at[b], sibling, lev)

    def anomaly(fl):
        block = cur[fl]
        sa[fl, 0:MEMBERS, :] = (block - jnp.mean(block, axis=0, keepdims=True)).astype(BF16)

    def cov(b, fl):
        for h in range(2):
            at = slice(256 * h, 256 * h + 256)
            got = dot(aj[...], sa[fl, :, at]) * locs[:, at]
            coef[fl, :, at] = got.astype(BF16)

    def change(b, fl):
        cur[fl] += dot(inc[b, 0:MEMBERS, :], coef[fl])

    def gather_z(b):
        wait_bytes(zr.at[b, pl.ds(0, NCOL - 1)], z_r.at[b])
        hi, lo = parts(zr[b].reshape(128, PAD), 2)
        return dot(cmat[b], hi) + dot(cmat[b], lo)

    def centred(v):
        mean = jnp.sum(v, axis=1, keepdims=True) * (1.0 / MEMBERS)
        return jnp.where(iota(v.shape, 1) < MEMBERS, v - mean, 0.0)

    prior = gather_z(0)
    for b in range(NB):
        anom = centred(prior)
        mine = pl.ds(pl.multiple_of(rho * 32, 32), 32)
        inn[b, mine, :] = jnp.where(in_members, ovs[b] - prior, 0.0).astype(BF16)
        spread(inn, b, wi_s, wi_r)
        variance = jnp.sum(anom * anom, axis=1, keepdims=True) / (MEMBERS - 1) + 1e-6
        scale = parts(1.0 / ((MEMBERS - 1) * variance), 3)
        for k in range(3):
            anom = jnp.where(lane_of == MEMBERS + k, scale[k].astype(F32), anom)
        an[b, mine, :] = anom.astype(BF16)
        spread(an, b, wa_s, wa_r)
        if b > 0:
            if b + 1 < NB:
                send_z(b + 1)
            loop(FL, lambda fl: change(b - 1, fl))
            loop(FL, anomaly)
        if b + 1 < NB:
            place(b + 1)
        forward(inn, b, wi_r, fi_s, fi_r)
        forward(an, b, wa_r, fa_s, fa_r)
        wait_bytes(inn.at[b, pl.ds(0, 512)], fi_r.at[b])
        rows = dot(gainp[b % 2], inn[b])
        lanes = pl.ds(pl.multiple_of(lev * 128, 128), 128)
        inc[b, 0:MEMBERS, lanes] = rows.T[0:MEMBERS].astype(BF16)

        def send_inc(k):
            piece = inc.at[b, pl.ds(0, MEMBERS), lanes]
            push(piece, piece, ic_s.at[b], ic_r.at[b], col, lev_peer(k))

        loop(NLEV - 1, send_inc)
        if b + 2 < NB:
            send_l(b + 1)
        wait_bytes(an.at[b, pl.ds(0, 512)], fa_r.at[b])

        def unpack(k):
            at = pl.ds(pl.multiple_of(k * 256, 256), 256)
            got = dot(perm[b % 2, at, :], an[b])
            scale_col = got[:, 80:81] + got[:, 81:82] + got[:, 82:83]
            aj[at, :] = got.astype(BF16)
            locs[at, :] = loc[b, at, :].astype(F32) * scale_col

        if b == NB - 1:
            loads[2 + b].wait()
        loop(4, unpack)
        if b + 1 < NB:
            after = 16 * (NB - 2 - b)
            held = gather_z(b + 1)
            wait_bytes(lrecv.at[b, pl.ds(0, NCOL - 1)], l_r.at[b])
            sel = dot(cbig[b], lrecv[b].reshape(NOBS, PAD))
            sel = jnp.concatenate([sel[32 * c:32 * c + 32] for c in range(8)], axis=1)
            if after:
                slots = own[b + 2:NB].reshape(after, PAD)
                held = jnp.concatenate([held, slots], axis=0)
                sel = jnp.concatenate([sel, later[b, 0:after, :]], axis=0)
            xh, xl = parts(centred(held), 2)
            pull = jnp.where((iota((16, PAD), 1) >= MEMBERS) & (iota((16, PAD), 1) < MEMBERS + 3), 1.0, 0.0).astype(BF16)
            count = 32 + after
            got = dot_nt(jnp.concatenate([xh, xl, pull], axis=0), aj[...])
            d = (got[0:count] + got[count:2 * count]) * got[2 * count:2 * count + 1] * sel
            dh, dl = parts(d, 2)
            dt[0:count, :] = dh
            dt[count:2 * count, :] = dl
        loop(FL, lambda fl: cov(b, fl))
        wait_bytes(inc.at[b, pl.ds(0, MEMBERS), pl.ds(0, 896)], ic_r.at[b])
        if b + 1 < NB:
            got = dot_nt(dt[0:2 * count, :], inc[b])
            held = held + got[0:count] + got[count:2 * count]
            prior = held[0:32]
            if after:
                own[b + 2:NB] = held[32:].reshape(NB - 2 - b, 16, PAD)
                for k in range(4):
                    zs[b + 2, k] = held[32 + 4 * k:36 + 4 * k]

    def finish(fl):
        block = cur[fl] + dot(inc[NB - 1, 0:MEMBERS, :], coef[fl])
        for c in range(4):
            raw[rows_of(fl, c), :] = block[:, 128 * c:128 * c + 128]

    loop(FL, finish)
    done = pltpu.make_async_copy(raw, out_hbm, out_sem)
    done.start()
    wait_bytes(rs.at[pl.ds(0, 7), 0], rs_s.at[0])
    wait_bytes(rs.at[pl.ds(0, 7), pl.ds(1, 3)], rs_s.at[1])
    for b in range(NB):
        wait_bytes(zr.at[b, pl.ds(0, NCOL - 1)], z_s.at[b])
        if b + 1 < NB:
            wait_bytes(lrecv.at[b, pl.ds(0, NCOL - 1)], l_s.at[b])
        wait_bytes(inn.at[b, pl.ds(0, 480)], wi_s.at[b])
        wait_bytes(an.at[b, pl.ds(0, 480)], wa_s.at[b])
        wait_bytes(inn.at[b, pl.ds(0, 512)], fi_s.at[b])
        wait_bytes(an.at[b, pl.ds(0, 512)], fa_s.at[b])
        wait_bytes(inc.at[b, pl.ds(0, MEMBERS), pl.ds(0, 896)], ic_s.at[b])
    done.wait()


def shards(ensemble, obs_weight, obs_value, obs_tile, obs_offset, obs_gain, localize):
    state = ensemble.reshape(MEMBERS, 4, 2, 4, 128).transpose(0, 1, 3, 2, 4).reshape(MEMBERS * 32, 128)
    weights = obs_weight.reshape(NB, 4, 2, 8, 128).transpose(0, 1, 3, 2, 4).reshape(NB * 64, 128)
    vmem, hbm = pl.BlockSpec(memory_space=pltpu.VMEM), pl.BlockSpec(memory_space=pl.ANY)
    dma = pltpu.SemaphoreType.DMA
    out = pl.pallas_call(
        kernel,
        out_shape=jax.ShapeDtypeStruct((MEMBERS * 32, 128), F32),
        in_specs=[vmem] * 4 + [hbm] * 3,
        out_specs=hbm,
        scratch_shapes=[
            pltpu.VMEM((MEMBERS * 32, 128), F32),
            pltpu.VMEM((FL, MEMBERS, WIDTH), F32),
            pltpu.VMEM((NB, 128, NOBS), BF16),
            pltpu.VMEM((NB, NOBS, WIDTH), BF16),
            pltpu.VMEM((WIDTH, NB * 128), BF16),
            pltpu.VMEM((PAD, NB * 128), F32),
            pltpu.VMEM((NB, NLEV, 16, PAD), F32),
            pltpu.VMEM((NB, PAD, 8), F32),
            pltpu.VMEM((NB, 16, PAD), F32),
            pltpu.VMEM((NLEV, NB, 16, PAD), F32),
            pltpu.VMEM((NB, 4, 4, PAD), F32),
            pltpu.VMEM((NB, NCOL, 4, PAD), F32),
            pltpu.VMEM((4, 8, 4, PAD), F32),
            pltpu.VMEM((NB - 1, 4, 32, PAD), BF16),
            pltpu.VMEM((NB - 1, NCOL, 32, PAD), BF16),
            pltpu.VMEM((2, 32, NOBS), F32),
            pltpu.VMEM((NB, NOBS, PAD), BF16),
            pltpu.VMEM((NB, NOBS, PAD), BF16),
            pltpu.VMEM((NB, PAD, NOBS), BF16),
            pltpu.VMEM((2, NOBS, NOBS), BF16),
            pltpu.VMEM((2, 128, NOBS), BF16),
            pltpu.VMEM((NOBS, PAD), BF16),
            pltpu.VMEM((NOBS, WIDTH), F32),
            pltpu.VMEM((128, NOBS), BF16),
            pltpu.VMEM((FL, PAD, WIDTH), BF16),
            pltpu.VMEM((FL, NOBS, WIDTH), BF16),
            pltpu.VMEM((NOBS, 8), F32),
            pltpu.VMEM((8, NB * 128), F32),
            pltpu.VMEM((NB, 32, 128), BF16),
            pltpu.VMEM((NB - 1, 256, NOBS), BF16),
            pltpu.VMEM((NB, 32, PAD), F32),
            dma((6,)), dma, dma((2,)), dma((2,)),
            dma((NB,)), dma((NB,)), dma((NB,)), dma((NB,)), dma((NB,)), dma((NB,)),
            dma((NB,)), dma((NB,)), dma((NB,)), dma((NB,)), dma((NB,)), dma((NB,)),
            dma((NB,)), dma((NB,)),
        ],
        compiler_params=pltpu.CompilerParams(
            collective_id=0, has_side_effects=True, vmem_limit_bytes=56 * 1024 * 1024),
        cost_estimate=pl.CostEstimate(flops=8 * 335544320, bytes_accessed=8 * 1024 * 1024, transcendentals=0),
    )(
        jnp.transpose(obs_tile, (0, 2, 1)), obs_offset, obs_value, weights, state, obs_gain, localize,
    )
    return out.reshape(MEMBERS, 4, 4, 2, 128).transpose(0, 1, 3, 2, 4).reshape(ensemble.shape)


def solution(mesh):
    in_specs = (
        P(None, None, "lev", "col"),
        P(None, None, "lev", None),
        P(),
        P(),
        P(),
        P(None, "lev", None),
        P(None, None, "col"),
    )
    out_specs = P(None, None, "lev", "col")
    return jax.shard_map(shards, mesh=mesh, in_specs=in_specs, out_specs=out_specs, check_vma=False)
```

time: 110 us -> 88 us (0.80)
  Pallas kernels: 100 us -> 85 us
  local copies, waits for them, and re-layouts: 9.48 us -> 2.83 us
    pallas_call x1, Pallas kernels: 100 us -> 85 us  [shards(): pl.pallas_call(kernel, out_shape=jax.ShapeDtypeStruct((MEMBERS * 32, 128)...]
    reshape x2 -> x0, local copies, waits for them, and re-layouts: 5.02 us -> none  [the longest x1 3.38 us: shards(): return jnp.transpose(out.reshape(4, 2, MEMBERS, WIDTH), (2, 0, 1, 3))]
    transpose x1 -> x0, local copies, waits for them, and re-layouts: 3.13 us -> none  [shards(): state = jnp.transpose(ensemble, (1, 2, 0, 3)).reshape(FL, MEMBERS, WIDTH)]
    unnamed x1, local copies, waits for them, and re-layouts: 1.32 us -> 2.83 us
where the time goes in v2:
time: 88 us; the launch traced here: 87.8 us
  Pallas kernels  85 us (97%)
  local copies, waits for them, and re-layouts  2.83 us (3%)
    pallas_call x1, Pallas kernels, shards(): pl.pallas_call(kernel, out_shape=jax.ShapeDtypeStruct((MEMBERS * 32, 128)...  85 us
    unnamed x1, local copies, waits for them, and re-layouts  2.83 us

profile of v2, /device:TPU:1, one launch (start us, length us, event | category | flops | bytes accessed | tf_op | source)
XLA Modules:
  0.0 87.8 jit_solution(808959060280578478)
XLA Ops:
  0.0 85.0 %shard_map.73 = f32[2560,128]{1,0:T(8,128)} custom-call(s32[4,1,1024]{2,1,0:T(1,128)} %bitcast.19, s32[4,1024]{1,0:T(4,128)} %off_ref.1, f32[4,1024]{1,0:T(4,128)} %val_ref.1, f32[256,128]{1,0:T(8,128)} %bitcast.18, f32[2560,128]{1,0:T(8,128)} %bitcast.17, bf16[4,128,1024]{2,1,0:T(8,128)(2,1)} %gain_hbm.1, bf16[4,1024,512]{2,1,0:T(8,128)(2,1)} %loc_hbm.1), custom_call_target="tpu_custom_call" | custom-call | flops 2684354560 | bytes 8388608 | tf_op jit(solution)/shard_map/pallas_call | solution.py:394
  85.0 2.8 %copy.12 = f32[80,4,2,512]{3,2,1,0:T(2,128)} copy(f32[80,4,2,512]{3,2,1,0:T(2,128)} %bitcast.16) | data formatting | bytes 2621440

commit v3 on v2

--- a/solution.py
+++ b/solution.py
@@ -47,8 +47,8 @@
         device_id={"col": col, "lev": lev}, device_id_type=MESH).start()
 
 
-def loop(count, body):
-    lax.fori_loop(0, count, lambda k, c: (body(k), c)[1], 0)
+def loop(count, body, unroll=1):
+    lax.fori_loop(0, count, lambda k, c: (body(k), c)[1], 0, unroll=unroll)
 
 
 def kernel(
@@ -56,7 +56,7 @@
     raw, cur, gain, loc, oh, x, xt, got_t, own, rs, zs, zr, ls, lsend, lrecv, later, inn, an, inc, perm, gainp,
     aj, locs, dt, sa, coef, gcol, wsl, cmat, cbig, ovs,
     in_sem, out_sem, rs_s, rs_r, z_s, z_r, l_s, l_r, wi_s, wi_r, wa_s, wa_r,
-    fi_s, fi_r, fa_s, fa_r, ic_s, ic_r,
+    fi_s, fi_r, fa_s, fa_r, ic_s, ic_r, lq_s, lq_r,
 ):
     col, lev = lax.axis_index("col"), lax.axis_index("lev")
     z, quad = col // 4, col % 4
@@ -71,21 +71,24 @@
     for load in loads:
         load.start()
 
-    def chip(k):
-        other = lax.rem(spot + k, 16)
-        return z * 4 + (other % 2) * 2 + core, other // 2
+    px, py = (lev % 2) * 2 + x_lo, lev // 2
+    plane = sorted([(dx, dy) for dx in range(4) for dy in range(4)], key=lambda d: -min(d[0], 4 - d[0]) - min(d[1], 4 - d[1]))[:15]
+
+    def moved(dx, dy):
+        tx, ty = (px + dx) % 4, (py + dy) % 4
+        return z * 4 + (tx % 2) * 2 + core, ty * 2 + tx // 2
+
+    chips = [moved(dx, dy) for dx, dy in plane]
+    lev_peers = [moved(dx, dy)[1] for dx, dy in plane if dx % 2 == 0]
 
     barrier = pltpu.get_barrier_semaphore()
 
     def greet_col(k):
         pl.semaphore_signal(barrier, inc=1, device_id={"col": lax.rem(col + k + 1, NCOL), "lev": lev}, device_id_type=MESH)
 
-    def greet_chip(k):
-        c, l = chip(k + 1)
+    loop(NCOL - 1, greet_col)
+    for c, l in chips:
         pl.semaphore_signal(barrier, inc=1, device_id={"col": c, "lev": l}, device_id_type=MESH)
-
-    loop(NCOL - 1, greet_col)
-    loop(15, greet_chip)
 
     tiles = [tile_ref[b] for b in range(NB)]
     member_of = jnp.concatenate(
@@ -145,25 +148,16 @@
         x[0:MEMBERS, :] += (got[0:80] + got[80:160] + got[160:240]) * wsl[pl.ds(fl, 1), :]
 
     sa[...] = jnp.zeros_like(sa)
-    loop(FL, project)
+    loop(FL, project, 2)
     for b in range(NB):
         xt[b] = x[:, 128 * b:128 * b + 128].T.reshape(NLEV, 16, PAD)
 
     pl.semaphore_wait(barrier, NCOL - 1 + 15)
 
-    def lev_peer(k):
-        return lax.rem(lev + k + 1, NLEV)
-
-    def send_first(k):
-        to = lev_peer(k)
+    for to in lev_peers:
         push(xt.at[0, to], rs.at[lev, 0], rs_s.at[0], rs_r.at[0], col, to)
-
-    def send_rest(k):
-        to = lev_peer(k)
+    for to in lev_peers:
         push(xt.at[pl.ds(1, 3), to], rs.at[lev, pl.ds(1, 3)], rs_s.at[1], rs_r.at[1], col, to)
-
-    loop(NLEV - 1, send_first)
-    loop(NLEV - 1, send_rest)
 
     gcol[...] = jnp.concatenate(g_rows + [jnp.zeros((4, NOBS), F32)], axis=0).T
     inc[...] = jnp.zeros_like(inc)
@@ -173,10 +167,10 @@
 
         def rows(k):
             at = pl.ds(pl.multiple_of(k * 256, 256), 256)
-            perm[b % 2, at, :] = jnp.where(gcol[at, b:b + 1] == want, 1.0, 0.0).astype(BF16)
-
-        loop(4, rows)
-        gainp[b % 2] = dot(gain[b], perm[b % 2]).astype(BF16)
+            perm[b, at, :] = jnp.where(gcol[at, b:b + 1] == want, 1.0, 0.0).astype(BF16)
+
+        loop(4, rows, 2)
+        gainp[b] = dot(gain[b], perm[b]).astype(BF16)
 
     loads[1].wait()
     place(0)
@@ -210,23 +204,27 @@
         is_here = g_rows[b].astype(I32) == 32 * iota((32, NOBS), 0) + rho
         ovs[b] = jnp.broadcast_to(jnp.sum(jnp.where(is_here, val_ref[b:b + 1, :], 0.0), axis=1, keepdims=True), (32, PAD))
 
+    def far_col(k):
+        return (col + 16 + ((k + 1) // 2) * (1 - 2 * (k % 2))) % NCOL
+
     def send_z(b):
         zr[b, col] = zs[b, quad]
 
         def one(k):
-            to = lax.rem(col + k + 1, NCOL)
+            to = far_col(k)
             push(zs.at[b, to % 4], zr.at[b, col], z_s.at[b], z_r.at[b], to, lev)
 
         loop(NCOL - 1, one)
 
+    lrecv[:, col] = lsend[:, quad]
+    for k in range(1, 4):
+        to = (quad + k) % 4
+        push(lsend.at[:, to], lrecv.at[:, col], lq_s, lq_r, z * 4 + to, lev)
+
     def send_l(b):
-        lrecv[b, col] = lsend[b, quad]
-
-        def one(k):
-            to = lax.rem(col + k + 1, NCOL)
-            push(lsend.at[b, to % 4], lrecv.at[b, col], l_s.at[b], l_r.at[b], to, lev)
-
-        loop(NCOL - 1, one)
+        piece = lrecv.at[b, pl.ds(z * 4, 4)]
+        for k in (4, 3, 5, 2, 6, 1, 7):
+            push(piece, piece, l_s.at[b], l_r.at[b], (z + k) % 8 * 4 + quad, lev)
 
     wait_bytes(rs.at[pl.ds(0, 7), 0], rs_r.at[0])
     rs[lev, 0] = xt[0, lev]
@@ -241,6 +239,7 @@
     for k in range(4):
         zs[1, k] = own[1, 4 * k:4 * k + 4]
     send_z(1)
+    wait_bytes(lrecv.at[:, pl.ds(0, 3)], lq_r)
     send_l(0)
 
     low, high = edges(NOBS, 32)
@@ -256,12 +255,8 @@
 
     def spread(buf, b, s_sem, r_sem):
         piece = buf.at[b, pl.ds(pl.multiple_of(rho * 32, 32), 32)]
-
-        def one(k):
-            c, l = chip(k + 1)
+        for c, l in chips:
             push(piece, piece, s_sem.at[b], r_sem.at[b], c, l)
-
-        loop(15, one)
 
     def forward(buf, b, r_sem, fs_sem, fr_sem):
         wait_bytes(buf.at[b, pl.ds(0, 480)], r_sem.at[b])
@@ -290,12 +285,14 @@
         mean = jnp.sum(v, axis=1, keepdims=True) * (1.0 / MEMBERS)
         return jnp.where(iota(v.shape, 1) < MEMBERS, v - mean, 0.0)
 
+    for b in range(1, NB):
+        place(b)
     prior = gather_z(0)
     for b in range(NB):
-        anom = centred(prior)
         mine = pl.ds(pl.multiple_of(rho * 32, 32), 32)
         inn[b, mine, :] = jnp.where(in_members, ovs[b] - prior, 0.0).astype(BF16)
         spread(inn, b, wi_s, wi_r)
+        anom = centred(prior)
         variance = jnp.sum(anom * anom, axis=1, keepdims=True) / (MEMBERS - 1) + 1e-6
         scale = parts(1.0 / ((MEMBERS - 1) * variance), 3)
         for k in range(3):
@@ -305,40 +302,38 @@
         if b > 0:
             if b + 1 < NB:
                 send_z(b + 1)
-            loop(FL, lambda fl: change(b - 1, fl))
-            loop(FL, anomaly)
-        if b + 1 < NB:
-            place(b + 1)
+            loop(FL, lambda fl: change(b - 1, fl), 4)
+            loop(FL, anomaly, 2)
         forward(inn, b, wi_r, fi_s, fi_r)
-        forward(an, b, wa_r, fa_s, fa_r)
+        near = pl.ds(pl.multiple_of(core * 512, 512), 512)
+        away = pl.ds(pl.multiple_of(512 - core * 512, 512), 512)
+        rows = dot(gainp[b, :, near], inn[b, near, :])
         wait_bytes(inn.at[b, pl.ds(0, 512)], fi_r.at[b])
-        rows = dot(gainp[b % 2], inn[b])
+        rows = rows + dot(gainp[b, :, away], inn[b, away, :])
         lanes = pl.ds(pl.multiple_of(lev * 128, 128), 128)
         inc[b, 0:MEMBERS, lanes] = rows.T[0:MEMBERS].astype(BF16)
-
-        def send_inc(k):
-            piece = inc.at[b, pl.ds(0, MEMBERS), lanes]
-            push(piece, piece, ic_s.at[b], ic_r.at[b], col, lev_peer(k))
-
-        loop(NLEV - 1, send_inc)
+        piece = inc.at[b, pl.ds(0, MEMBERS), lanes]
+        for to in lev_peers:
+            push(piece, piece, ic_s.at[b], ic_r.at[b], col, to)
+        forward(an, b, wa_r, fa_s, fa_r)
         if b + 2 < NB:
             send_l(b + 1)
         wait_bytes(an.at[b, pl.ds(0, 512)], fa_r.at[b])
 
         def unpack(k):
             at = pl.ds(pl.multiple_of(k * 256, 256), 256)
-            got = dot(perm[b % 2, at, :], an[b])
+            got = dot(perm[b, at, :], an[b])
             scale_col = got[:, 80:81] + got[:, 81:82] + got[:, 82:83]
             aj[at, :] = got.astype(BF16)
             locs[at, :] = loc[b, at, :].astype(F32) * scale_col
 
         if b == NB - 1:
             loads[2 + b].wait()
-        loop(4, unpack)
+        loop(4, unpack, 4)
         if b + 1 < NB:
             after = 16 * (NB - 2 - b)
             held = gather_z(b + 1)
-            wait_bytes(lrecv.at[b, pl.ds(0, NCOL - 1)], l_r.at[b])
+            wait_bytes(lrecv.at[b, pl.ds(0, 28)], l_r.at[b])
             sel = dot(cbig[b], lrecv[b].reshape(NOBS, PAD))
             sel = jnp.concatenate([sel[32 * c:32 * c + 32] for c in range(8)], axis=1)
             if after:
@@ -353,7 +348,7 @@
             dh, dl = parts(d, 2)
             dt[0:count, :] = dh
             dt[count:2 * count, :] = dl
-        loop(FL, lambda fl: cov(b, fl))
+        loop(FL, lambda fl: cov(b, fl), 4)
         wait_bytes(inc.at[b, pl.ds(0, MEMBERS), pl.ds(0, 896)], ic_r.at[b])
         if b + 1 < NB:
             got = dot_nt(dt[0:2 * count, :], inc[b])
@@ -369,15 +364,16 @@
         for c in range(4):
             raw[rows_of(fl, c), :] = block[:, 128 * c:128 * c + 128]
 
-    loop(FL, finish)
+    loop(FL, finish, 4)
     done = pltpu.make_async_copy(raw, out_hbm, out_sem)
     done.start()
     wait_bytes(rs.at[pl.ds(0, 7), 0], rs_s.at[0])
     wait_bytes(rs.at[pl.ds(0, 7), pl.ds(1, 3)], rs_s.at[1])
+    wait_bytes(lrecv.at[:, pl.ds(0, 3)], lq_s)
     for b in range(NB):
         wait_bytes(zr.at[b, pl.ds(0, NCOL - 1)], z_s.at[b])
         if b + 1 < NB:
-            wait_bytes(lrecv.at[b, pl.ds(0, NCOL - 1)], l_s.at[b])
+            wait_bytes(lrecv.at[b, pl.ds(0, 28)], l_s.at[b])
         wait_bytes(inn.at[b, pl.ds(0, 480)], wi_s.at[b])
         wait_bytes(an.at[b, pl.ds(0, 480)], wa_s.at[b])
         wait_bytes(inn.at[b, pl.ds(0, 512)], fi_s.at[b])
@@ -416,8 +412,8 @@
             pltpu.VMEM((NB, NOBS, PAD), BF16),
             pltpu.VMEM((NB, NOBS, PAD), BF16),
             pltpu.VMEM((NB, PAD, NOBS), BF16),
-            pltpu.VMEM((2, NOBS, NOBS), BF16),
-            pltpu.VMEM((2, 128, NOBS), BF16),
+            pltpu.VMEM((NB, NOBS, NOBS), BF16),
+            pltpu.VMEM((NB, 128, NOBS), BF16),
             pltpu.VMEM((NOBS, PAD), BF16),
             pltpu.VMEM((NOBS, WIDTH), F32),
             pltpu.VMEM((128, NOBS), BF16),
@@ -431,7 +427,7 @@
             dma((6,)), dma, dma((2,)), dma((2,)),
             dma((NB,)), dma((NB,)), dma((NB,)), dma((NB,)), dma((NB,)), dma((NB,)),
             dma((NB,)), dma((NB,)), dma((NB,)), dma((NB,)), dma((NB,)), dma((NB,)),
-            dma((NB,)), dma((NB,)),
+            dma((NB,)), dma((NB,)), dma, dma,
         ],
         compiler_params=pltpu.CompilerParams(
             collective_id=0, has_side_effects=True, vmem_limit_bytes=56 * 1024 * 1024),

time: 88 us -> 76.4 us (0.87)
  Pallas kernels: 85 us -> 73.4 us
    pallas_call x1, Pallas kernels: 85 us -> 73.4 us  [shards(): pl.pallas_call(kernel, out_shape=jax.ShapeDtypeStruct((MEMBERS * 32, 128)...]
where the time goes in v3:
time: 76.4 us; the launch traced here: 76.2 us
  Pallas kernels  73.4 us (96%)
  local copies, waits for them, and re-layouts  2.83 us (4%)
    pallas_call x1, Pallas kernels, shards(): pl.pallas_call(kernel, out_shape=jax.ShapeDtypeStruct((MEMBERS * 32, 128)...  73.4 us
    unnamed x1, local copies, waits for them, and re-layouts  2.83 us

profile of v3, /device:TPU:1, one launch (start us, length us, event | category | flops | bytes accessed | tf_op | source)
XLA Modules:
  0.0 76.2 jit_solution(16891987164103448749)
XLA Ops:
  0.0 73.4 %shard_map.73 = f32[2560,128]{1,0:T(8,128)} custom-call(s32[4,1,1024]{2,1,0:T(1,128)} %bitcast.19, s32[4,1024]{1,0:T(4,128)} %off_ref.1, f32[4,1024]{1,0:T(4,128)} %val_ref.1, f32[256,128]{1,0:T(8,128)} %bitcast.18, f32[2560,128]{1,0:T(8,128)} %bitcast.17, bf16[4,128,1024]{2,1,0:T(8,128)(2,1)} %gain_hbm.1, bf16[4,1024,512]{2,1,0:T(8,128)(2,1)} %loc_hbm.1), custom_call_target="tpu_custom_call" | custom-call | flops 2684354560 | bytes 8388608 | tf_op jit(solution)/shard_map/pallas_call | solution.py:390
  73.4 2.8 %copy.12 = f32[80,4,2,512]{3,2,1,0:T(2,128)} copy(f32[80,4,2,512]{3,2,1,0:T(2,128)} %bitcast.16) | data formatting | bytes 2621440
